TPU v7x, 32 devices: a whole 2x2x4 slice. The times are simulated.
32 devices in a mesh: gr: 4 (over y, x), gc: 8 (over z, core).
Axes of the slice: x: 2, y: 2, z: 4, core: 2. Of those that a mesh axis runs over, the one named last changes fastest.
Arguments:
- phase: bfloat16 [2, 12288, 512], P(None, 'gr', 'gc'), may hold values from -0.59765625 to 0.59765625
- data: bfloat16 [2, 512, 128], P(None, 'gc'), may hold values from -6 to 6
- column_ids: int32 [512], replicated, may hold values from 0 to 8191
- noise_weight: float32 [8192], replicated, may hold values from 0.3 to 3
Outputs:
- fisher: float32 [12288, 12288], P('gr', 'gc')
- dirty_maps: float32 [12288, 128], P(('gr', 'gc'))
All inputs are finite; a program needn't handle non-finite values.
Results may differ from a plain program's by a relative error of at most 0.0029.
Values may be sent and summed in bfloat16 or wider, within the bound.
A program may use at most 128 MiB of HBM per device.

v0:
```python
import jax
import jax.numpy as jnp
from jax import lax
from jax.sharding import PartitionSpec as P


def from_root(block, axis, source):
    block = jnp.where(lax.axis_index(axis) == source, block, jnp.zeros_like(block))
    return lax.psum(block, axis)


def shards(phase, data, column_ids, noise_weight):
    grid_rows = lax.axis_size("gr")
    grid_cols = lax.axis_size("gc")
    col_index = lax.axis_index("gc")
    left_count = phase.shape[1]
    right_count = left_count * grid_rows // grid_cols
    ratio = grid_cols // grid_rows
    weight = jnp.take(noise_weight, column_ids)
    left = lax.all_gather(phase, "gc", axis=2, tiled=True)
    offset = col_index % ratio * right_count
    root = col_index // ratio
    piece = lax.dynamic_slice_in_dim(left, offset, right_count, 1)
    received = from_root(piece, "gr", root)
    weighted_right = (received.astype(jnp.float32) * weight).astype(jnp.bfloat16)
    fisher = lax.dot_general(
        left, weighted_right, (((0, 2), (0, 2)), ((), ())), preferred_element_type=jnp.float32
    )
    owned = left_count // grid_cols
    own_rows = lax.dynamic_slice_in_dim(left, col_index * owned, owned, 1)
    weighted_own = (own_rows.astype(jnp.float32) * weight).astype(jnp.bfloat16)
    all_data = lax.all_gather(data, "gc", axis=1, tiled=True)
    dirty_maps = lax.dot_general(
        weighted_own, all_data, (((0, 2), (0, 1)), ((), ())), preferred_element_type=jnp.float32
    )
    return (fisher, dirty_maps)


def solution(mesh):
    return jax.shard_map(
        shards,
        mesh=mesh,
        in_specs=(P(None, "gr", "gc"), P(None, "gc", None), P(), P()),
        out_specs=(P("gr", "gc"), P(("gr", "gc"), None)),
        check_vma=False,
    )
```

profile of v0, /device:TPU:3, one launch (start us, length us, event | category | flops | bytes accessed | tf_op | source)
XLA Modules:
  0.0 208.3 jit_solution(8750557164308945706)
XLA Ops:
  7.2 0.0 copy-start
  7.2 0.0 copy-start.2
  7.2 0.0 copy-start.1
  7.2 0.0 all-gather.2.cloned.1.call-start
  7.2 0.7 all-gather.2.cloned.1.call-update
  7.9 0.0 all-reduce.2.cloned.1.call-start
  8.0 68.0 %all-gather.2.cloned.1.call-done = bf16[2,3072,512]{1,2,0:T(8,128)(2,1)} async-done(((bf16[2,3072,64]{1,2,0:T(8,128)(2,1)}), bf16[2,3072,512]{1,2,0:T(8,128)(2,1)}) %all-gather.2.cloned.1.call-update) | async-done | bytes 6291472 | tf_op jit(solution)/shard_map/all_gather | solution.py:20
  76.0 4.1 %dynamic-slice_select_fusion = bf16[2,1536,512]{1,2,0:T(8,128)(2,1)} fusion(bf16[2,3072,512]{1,2,0:T(8,128)(2,1)} %all-gather.2.cloned.1.call-done, s32[]{:T(128)S(6)} %select_n.39, pred[]{:T(512)S(6)} %eq.5), kind=kLoop, calls=%fused_computation.4 | loop fusion | flops 1572864 | bytes 6291461 | tf_op jit(solution)/shard_map/jit(_where)/select_n | solution.py:8
  80.1 0.0 all-reduce.2.cloned.1.call-update
  80.1 0.0 copy-done.2
  80.2 0.0 copy-done
  80.2 3.1 %gather_fusion = f32[512]{0:T(512)S(1)} fusion(f32[8192]{0:T(1024)S(1)} %copy-done, s32[1024]{0:T(1024)S(1)} %pad_clamp_fusion), kind=kCustom, calls=%fused_computation | custom fusion | bytes 6144 | tf_op jit(solution)/shard_map/jit(_take)/gather | solution.py:19
  83.3 0.0 copy-done.1
  83.3 14.3 %all_gather.7 = bf16[2,512,128]{2,1,0:T(8,128)(2,1)S(1)} all-gather(bf16[2,64,128]{2,1,0:T(8,128)(2,1)S(1)} %copy-done.1), channel_id=1, replica_groups=mesh['gr'=4,'gc'=8] {'gc'}, dimensions={1}, use_global_device_ids=true | all-gather | bytes 294912 | tf_op jit(solution)/shard_map/all_gather | solution.py:32
  97.6 2.4 %convolution_bitcast_fusion.1 = f32[384,128]{1,0:T(8,128)} fusion(bf16[2,512,128]{2,1,0:T(8,128)(2,1)S(1)} %all_gather.7, f32[512]{0:T(512)S(1)} %and_select_fusion, bf16[2,3072,512]{1,2,0:T(8,128)(2,1)} %all-gather.2.cloned.1.call-done, s32[]{:T(128)S(6)} %select_n.43), kind=kOutput, calls=%fused_computation.6 | convolution fusion | flops 101842944 | bytes 1247236 | tf_op jit(solution)/shard_map/dot_general | solution.py:33
  100.0 65.8 %all-reduce.2.cloned.1.call-done = bf16[2,1536,512]{1,2,0:T(8,128)(2,1)} async-done(((bf16[2,1536,512]{1,2,0:T(8,128)(2,1)}), bf16[2,1536,512]{1,2,0:T(8,128)(2,1)}) %all-reduce.2.cloned.1.call-update) | async-done | bytes 3145744 | tf_op jit(solution)/shard_map/psum | solution.py:9
  165.8 17.1 %convolution_bitcast_fusion = f32[3072,1536]{0,1:T(8,128)} fusion(bf16[2,3072,512]{1,2,0:T(8,128)(2,1)} %all-gather.2.cloned.1.call-done, bf16[2,1536,512]{1,2,0:T(8,128)(2,1)} %all-reduce.2.cloned.1.call-done, f32[512]{0:T(512)S(1)} %and_select_fusion), kind=kOutput, calls=%fused_computation.1 | convolution fusion | flops 9668395008 | bytes 28313600 | tf_op jit(solution)/shard_map/dot_general | solution.py:26
  182.9 18.6 %copy.11 = f32[3072,1536]{1,0:T(8,128)} copy(f32[3072,1536]{0,1:T(8,128)} %convolution_bitcast_fusion) | data formatting | bytes 37748736
  (3 shorter events, 0.0 us)
Async XLA Ops:
  7.2 73.0 %copy-start = (f32[8192]{0:T(1024)S(1)}, f32[8192]{0:T(1024)}, u32[]{:S(2)}) copy-start(f32[8192]{0:T(1024)} %param.7) | copy-start | bytes 98308
  7.2 73.0 %copy-start.2 = (s32[512]{0:T(512)S(1)}, s32[512]{0:T(512)}, u32[]{:S(2)}) copy-start(s32[512]{0:T(512)} %param.6) | copy-start | bytes 6148
  7.2 76.2 %copy-start.1 = (bf16[2,64,128]{2,1,0:T(8,128)(2,1)S(1)}, bf16[2,64,128]{2,1,0:T(8,128)(2,1)}, u32[]{:S(2)}) copy-start(bf16[2,64,128]{2,1,0:T(8,128)(2,1)} %param.5) | copy-start | bytes 98308
  7.2 68.8 %all-gather.2.cloned.1.call-start = ((), (), s32[]{:S(2)}) async-start(), calls=%async_computation | async-start | bytes 7077888 | tf_op jit(solution)/shard_map/all_gather | solution.py:20
  7.9 157.8 %all-reduce.2.cloned.1.call-start = ((), (), s32[]{:S(2)}) async-start(), calls=%async_computation.1 | async-start | bytes 6291456 | tf_op jit(solution)/shard_map/psum | solution.py:9
Sparse Core Ops, SparseCore 0:
  9.6 66.3 all-gather.1
  80.3 85.4 all-reduce.1
where the time goes:
time: 210 us; the launch traced here: 208 us
  waiting for transfers between devices  134 us (64%)
  local copies, waits for them, and re-layouts  21.8 us (10%)
  matrix products  19.4 us (9%)
  blocking collectives  14.3 us (7%)
  between operations  14.1 us (7%)
  other arithmetic  4.1 us (2%)
    all_gather x1, waiting for transfers between devices, shards(): left = lax.all_gather(phase, 'gc', axis=2, tiled=True)  68 us
    psum x1, waiting for transfers between devices, from_root(): return lax.psum(block, axis)  65.8 us
    unnamed x7, local copies, waits for them, and re-layouts  18.7 us
    dot_general x1, matrix products, shards(): lax.dot_general(left, weighted_right, (((0, 2), (0, 2)), ((), ())), prefe...  17.1 us
    all_gather x1, blocking collectives, shards(): all_data = lax.all_gather(data, 'gc', axis=1, tiled=True)  14.3 us
  transfers between devices with their start and end apart: 2, of which 2 were waited for; matrix products, arithmetic and copies ran while one was open for 3% of the time, Pallas kernels for 0%

commit v1 on v0

v1 whole, which is shorter than its diff:
```python
import functools
import math

import jax
import jax.numpy as jnp
from jax import lax
from jax.experimental import pallas as pl
from jax.experimental.pallas import tpu as pltpu
from jax.sharding import PartitionSpec as P

MESH = pl.DeviceIdType.MESH


def gather_kernel(
    G, C, rows, phase_ref, data_ref, left, right, own,
    up_sem, down_sem, twin_sem, root_sem, ring_sem, keep_sem, own_sem, got, got_right,
):
    Z = C // 2
    pixels = phase_ref.shape[1]
    half = phase_ref.shape[2]
    extra = data_ref.shape[0] * data_ref.shape[1]
    Q = right.shape[1]
    parts = Q // rows
    S = 2 * parts
    g, d = lax.axis_index("gr"), lax.axis_index("gc")
    z, c = d // 2, d % 2
    other = 1 - c
    gy, gx = g // 2, g % 2
    pos = (1 - gx) * gy + gx * (G - 1 - gy)
    ry, rx = z // 2, z % 2
    turn = (pos - ((1 - rx) * ry + rx * (G - 1 - ry)) + G) % G
    is_root = turn == 0

    def ring_device(at):
        at = at % G
        far = at // (G // 2)
        return (1 - far) * 2 * at + far * (2 * (G - 1 - at) + 1)

    ahead, behind = ring_device(pos + 1), ring_device(pos + G - 1)
    send_way = (1 - c) * ahead + c * behind
    not_first, not_last = z > 0, z < Z - 1

    barrier = pltpu.get_barrier_semaphore()

    def greet(device):
        pl.semaphore_signal(barrier, inc=1, device_id=device, device_id_type=MESH)

    greet((g, 2 * z + other))
    for core in range(2):
        greet((ahead, 2 * z + core))
        greet((behind, 2 * z + core))

    @pl.when(not_last)
    def _():
        greet((g, d + 2))

    @pl.when(not_first)
    def _():
        greet((g, d - 2))

    pl.semaphore_wait(barrier, 5 + not_last.astype(jnp.int32) + not_first.astype(jnp.int32))

    def remote(src, dst, send_sem, recv_sem, device):
        return pltpu.make_async_remote_copy(
            src_ref=src, dst_ref=dst, send_sem=send_sem, recv_sem=recv_sem, device_id=device, device_id_type=MESH
        )

    def arrived(piece, sem):
        remote(piece, piece, own_sem, sem, (g, d)).wait_recv()

    def spread(src, zb, block, cut, sem):
        dst = left.at[block, cut]

        @pl.when((zb <= z) & not_last)
        def _():
            remote(src, dst, up_sem.at[zb], sem, (g, d + 2)).start()

        @pl.when((zb >= z) & not_first)
        def _():
            remote(src, dst, down_sem.at[zb], sem, (g, d - 2)).start()

        remote(src, dst, twin_sem.at[zb], sem, (g, 2 * z + other)).start()

    def start_of(m):
        return pl.multiple_of((m % 2) * Q + (m // 2) * rows, rows)

    def broadcast(src, zb, block, m):
        at = pl.multiple_of((m // 2) * rows, rows)
        remote(
            src, right.at[block, pl.ds(at, rows)], root_sem.at[zb], got_right.at[block, m // 2],
            (send_way, 2 * z + m % 2),
        ).start()

    def keep(src, block, m):
        at = pl.multiple_of((m // 2) * rows, rows)
        pltpu.make_async_copy(src, right.at[block, pl.ds(at, rows)], keep_sem.at[block]).start()

    tail = pl.ds(pixels, extra)
    own[pl.ds(pixels, half)] = data_ref[0]
    own[pl.ds(pixels + half, half)] = data_ref[1]
    spread(own.at[tail], z, d, tail, got.at[d, S])
    pltpu.make_async_copy(own.at[tail], left.at[d, tail], own_sem).start()

    def step(s, carry):
        @pl.when(s < S)
        def _():
            at = start_of(s)
            cut = pl.ds(at, rows)
            own[cut] = jnp.concatenate([phase_ref[0, cut], phase_ref[1, cut]], axis=1)
            spread(own.at[cut], z, d, cut, got.at[d, s])
            pltpu.make_async_copy(own.at[cut], left.at[d, cut], own_sem).start()

            @pl.when(is_root)
            def _():
                broadcast(own.at[cut], z, d, s)

                @pl.when(s % 2 == c)
                def _():
                    keep(own.at[cut], d, s)

        for zb in range(Z):
            away = jnp.maximum(zb - z, z - zb)
            mine, twin = 2 * zb + c, 2 * zb + other
            m = s - away

            @pl.when((zb != z) & (m >= 0) & (m < S))
            def _():
                cut = pl.ds(start_of(m), rows)
                piece = left.at[mine, cut]
                arrived(piece, got.at[mine, m])
                spread(piece, zb, mine, cut, got.at[mine, m])

                @pl.when(is_root)
                def _():
                    broadcast(piece, zb, mine, m)

                    @pl.when(m % 2 == c)
                    def _():
                        keep(piece, mine, m)

            @pl.when((zb != z) & (s == away))
            def _():
                arrived(left.at[mine, tail], got.at[mine, S])
                spread(left.at[mine, tail], zb, mine, tail, got.at[mine, S])

            n = s - away - 1

            @pl.when((n >= 0) & (n < S))
            def _():
                piece = left.at[twin, pl.ds(start_of(n), rows)]
                arrived(piece, got.at[twin, n])

                @pl.when(is_root & (n % 2 == c))
                def _():
                    keep(piece, twin, n)

            for e in range(2):
                hops = turn if e == 0 else G - turn
                r = s - away - hops

                @pl.when((turn > 0) & (r >= 0) & (r < S) & (r % 2 == c))
                def _():
                    block = 2 * zb + e
                    piece = right.at[block, pl.ds(pl.multiple_of((r // 2) * rows, rows), rows)]
                    arrived(piece, got_right.at[block, r // 2])

                    @pl.when(hops < G - 1)
                    def _():
                        remote(
                            piece, piece, ring_sem.at[block], got_right.at[block, r // 2],
                            (ahead if e == 0 else behind, d),
                        ).start()

        return carry

    lax.fori_loop(0, S + Z - 1 + G, step, 0)

    def sent(piece, sem):
        remote(piece, piece, sem, got.at[0, 0], (g, d)).wait_send()

    for zb in range(Z):
        mine, twin = 2 * zb + c, 2 * zb + other
        arrived(left.at[twin, tail], got.at[twin, S])
        sent(left.at[mine], twin_sem.at[zb])

        @pl.when((zb <= z) & not_last)
        def _():
            sent(left.at[mine], up_sem.at[zb])

        @pl.when((zb >= z) & not_first)
        def _():
            sent(left.at[mine], down_sem.at[zb])

        @pl.when(is_root)
        def _():
            sent(left.at[mine, pl.ds(0, pixels)], root_sem.at[zb])

        for e in range(2):
            block = 2 * zb + e
            hops = turn if e == 0 else G - turn

            @pl.when(is_root)
            def _():
                pltpu.make_async_copy(right.at[block], right.at[block], keep_sem.at[block]).wait()

            @pl.when((turn > 0) & (hops < G - 1))
            def _():
                sent(right.at[block], ring_sem.at[block])

    pltpu.make_async_copy(own, left.at[d], own_sem).wait()


def gather(phase, data, G, C):
    _, pixels, half = phase.shape
    extra = 2 * half
    Z = C // 2
    Q = pixels * G // C
    rows = math.gcd(Q, 192)
    dma = pltpu.SemaphoreType.DMA
    return pl.pallas_call(
        functools.partial(gather_kernel, G, C, rows),
        out_shape=(
            jax.ShapeDtypeStruct((C, pixels + extra, 2 * half), jnp.bfloat16),
            jax.ShapeDtypeStruct((C, Q, 2 * half), jnp.bfloat16),
        ),
        in_specs=[pl.BlockSpec(memory_space=pltpu.VMEM)] * 2,
        out_specs=(pl.BlockSpec(memory_space=pl.ANY),) * 2,
        scratch_shapes=[
            pltpu.VMEM((pixels + extra, 2 * half), jnp.bfloat16),
            dma((Z,)), dma((Z,)), dma((Z,)), dma((Z,)), dma((C,)), dma((C,)), dma,
            dma((C, 2 * (Q // rows) + 1)), dma((C, Q // rows)),
        ],
        compiler_params=pltpu.CompilerParams(
            collective_id=0, has_side_effects=True, vmem_limit_bytes=48 * 2**20
        ),
    )(phase, data)


def product_kernel(where, left, right, own, data, scale, fisher, maps, weighted):
    C = left.shape[0]
    width = left.shape[2]

    def scaled(ref, b):
        return (ref[b].astype(jnp.float32) * scale[b]).astype(jnp.bfloat16)

    @pl.when(pl.program_id(0) == 0)
    def _():
        for b in range(C):
            weighted[:, b * width:(b + 1) * width] = scaled(right, b)

    rows = jnp.concatenate([left[b] for b in range(C)], axis=1)
    fisher[...] = lax.dot_general(
        rows, weighted[...], (((1,), (1,)), ((), ())), preferred_element_type=jnp.float32
    )

    @pl.when(pl.program_id(0) == pl.num_programs(0) - 1)
    def _():
        mine = jnp.concatenate([scaled(own, b) for b in range(C)], axis=1)
        columns = jnp.concatenate([data[b] for b in range(C)], axis=0)
        maps[...] = jnp.dot(mine, columns, preferred_element_type=jnp.float32)


def shards(phase, data, column_ids, noise_weight):
    G, C = lax.axis_size("gr"), lax.axis_size("gc")
    _, pixels, half = phase.shape
    width = 2 * half
    Q = pixels * G // C
    owned = pixels // C
    maps = data.shape[2]
    weight = jnp.take(noise_weight, column_ids).reshape(C, 1, half)
    scale = jnp.concatenate([weight, weight], axis=2)
    left, right = gather(phase, data, G, C)
    tile = math.gcd(pixels, 256)
    once = pl.Buffered(1)
    where = lax.axis_index("gc").astype(jnp.int32).reshape(1)
    return pl.pallas_call(
        product_kernel,
        grid_spec=pltpu.PrefetchScalarGridSpec(
            num_scalar_prefetch=1,
            grid=(pixels // tile,),
            in_specs=[
                pl.BlockSpec((C, tile, width), lambda i, at: (0, i, 0)),
                pl.BlockSpec((C, Q, width), lambda i, at: (0, 0, 0), pipeline_mode=once),
                pl.BlockSpec((C, owned, width), lambda i, at: (0, at[0], 0), pipeline_mode=once),
                pl.BlockSpec((C, width, maps), lambda i, at: (0, pixels // width, 0), pipeline_mode=once),
                pl.BlockSpec((C, 1, width), lambda i, at: (0, 0, 0), pipeline_mode=once),
            ],
            out_specs=[
                pl.BlockSpec((tile, Q), lambda i, at: (i, 0)),
                pl.BlockSpec((owned, maps), lambda i, at: (0, 0)),
            ],
            scratch_shapes=[pltpu.VMEM((Q, C * width), jnp.bfloat16)],
        ),
        out_shape=(
            jax.ShapeDtypeStruct((pixels, Q), jnp.float32),
            jax.ShapeDtypeStruct((owned, maps), jnp.float32),
        ),
        compiler_params=pltpu.CompilerParams(vmem_limit_bytes=48 * 2**20),
    )(where, left, right, left, left, scale)


def solution(mesh):
    return jax.shard_map(
        shards,
        mesh=mesh,
        in_specs=(P(None, "gr", "gc"), P(None, "gc", None), P(), P()),
        out_specs=(P("gr", "gc"), P(("gr", "gc"), None)),
        check_vma=False,
    )
```

time: 210 us -> 101 us (0.48)
  waiting for transfers between devices: 134 us -> 0 us
  Pallas kernels: 0 us -> 92.6 us
  matrix products: 19.4 us -> 0 us
  local copies, waits for them, and re-layouts: 21.8 us -> 5.8 us
  blocking collectives: 14.3 us -> 0 us
  between operations: 14.1 us -> 0.68 us
  other arithmetic: 4.1 us -> 1.46 us
    pallas_call x0 -> x2, Pallas kernels: none -> 92.6 us  [the longest x1 74 us: gather(): pl.pallas_call(functools.partial(gather_kernel, G, C, rows), out_shape=(j...]
    all_gather x1 -> x0, waiting for transfers between devices: 68 us -> none  [shards(): left = lax.all_gather(phase, 'gc', axis=2, tiled=True)]
    psum x1 -> x0, waiting for transfers between devices: 65.8 us -> none  [from_root(): return lax.psum(block, axis)]
    dot_general x2 -> x0, matrix products: 19.4 us -> none  [the longest x1 17.1 us: shards(): lax.dot_general(left, weighted_right, (((0, 2), (0, 2)), ((), ())), prefe...]
    unnamed x7 -> x5, local copies, waits for them, and re-layouts: 18.7 us -> 2.59 us
    all_gather x1 -> x0, blocking collectives: 14.3 us -> none  [shards(): all_data = lax.all_gather(data, 'gc', axis=1, tiled=True)]
    select_n x3 -> x2, other arithmetic: 4.1 us -> 1.38 us  [shards(): weight = jnp.take(noise_weight, column_ids).reshape(C, 1, half)]
  transfers between devices with their start and end apart: 2 -> 0, of which waited for: 2 -> 0; matrix products, arithmetic and copies ran while one was open for 3% -> 0% of each run, Pallas kernels for 0% -> 0%
where the time goes in v1:
time: 101 us
  Pallas kernels  92.6 us (92%)
  local copies, waits for them, and re-layouts  5.8 us (6%)
  other arithmetic  1.46 us (1%)
    pallas_call x1, Pallas kernels, gather(): pl.pallas_call(functools.partial(gather_kernel, G, C, rows), out_shape=(j...  74 us
    pallas_call x1, Pallas kernels, shards(): pl.pallas_call(product_kernel, grid_spec=pltpu.PrefetchScalarGridSpec(num...  18.6 us
    gather x1, local copies, waits for them, and re-layouts, shards(): weight = jnp.take(noise_weight, column_ids).reshape(C, 1, half)  3.13 us
    unnamed x5, local copies, waits for them, and re-layouts  2.59 us

profile of v1, /device:TPU:3, one launch (start us, length us, event | category | flops | bytes accessed | tf_op | source)
XLA Modules:
  0.0 100.6 jit_solution(5230996699262577076)
XLA Ops:
  0.6 0.0 copy-start
  0.6 0.7 compare_select_fusion
  1.3 0.0 copy-done
  1.4 3.1 %gather_fusion = f32[512]{0:T(512)S(1)} fusion(f32[8192]{0:T(1024)S(1)} %copy-done, s32[1024]{0:T(1024)S(1)} %pad_clamp_fusion), kind=kCustom, calls=%fused_computation | custom fusion | bytes 6144 | tf_op jit(solution)/shard_map/jit(_take)/gather | solution.py:270
  4.5 0.7 and_select_fusion
  5.2 0.1 select_n.21
  5.3 0.1 pad_maximum_fusion.scale
  5.4 1.8 %copy.7.phase_ref = bf16[2,3072,64]{2,1,0:T(8,128)(2,1)S(1)} copy(bf16[2,3072,64]{1,2,0:T(8,128)(2,1)} %param.4) | data formatting | bytes 1572864 | tf_op args[0]
  7.2 0.0 copy-start.1
  7.2 0.7 copy-done.1
  7.9 74.0 %shard_map.59 = (bf16[8,3200,128]{2,1,0:T(8,128)(2,1)}, bf16[8,1536,128]{2,1,0:T(8,128)(2,1)S(1)}) custom-call(bf16[2,3072,64]{2,1,0:T(8,128)(2,1)S(1)} %copy.7.phase_ref, bf16[2,64,128]{2,1,0:T(8,128)(2,1)S(1)} %copy-done.1), custom_call_target="tpu_custom_call" | custom-call | tf_op jit(solution)/shard_map/pallas_call | solution.py:220
  81.9 18.6 %shard_map.60 = (f32[3072,1536]{1,0:T(8,128)}, f32[384,128]{1,0:T(8,128)}) custom-call(s32[1]{0:T(128)} %bitcast.where, bf16[8,3200,128]{2,1,0:T(8,128)(2,1)} %get-tuple-element.4.left.own.data, bf16[8,1536,128]{2,1,0:T(8,128)(2,1)S(1)} %get-tuple-element.5.right, bf16[8,3200,128]{2,1,0:T(8,128)(2,1)} %get-tuple-element.4.left.own.data, ...), custom_call_target="tpu_custom_call" | custom-call | tf_op jit(solution)/shard_map/pallas_call | solution.py:276
  (1 shorter events, 0.0 us)
Async XLA Ops:
  0.6 0.8 copy-start
  7.2 0.8 copy-start.1

commit v2 on v1

v2 whole, which is shorter than its diff:
```python
import functools
import math

import jax
import jax.numpy as jnp
from jax import lax
from jax.experimental import pallas as pl
from jax.experimental.pallas import tpu as pltpu
from jax.sharding import PartitionSpec as P

MESH = pl.DeviceIdType.MESH


def sky_kernel(
    G, C, rows, phase_ref, data_ref, ids_ref, table_ref, fisher, maps, left, right, weighted, scale, spare,
    up_sem, down_sem, twin_sem, root_sem, ring_sem, got, got_right,
):
    Z = C // 2
    half, pixels = phase_ref.shape[1:]
    width = 2 * half
    extra = data_ref.shape[0] * data_ref.shape[1]
    Q = right.shape[1]
    owned = pixels // C
    parts = Q // rows
    S = 2 * parts
    g, d = lax.axis_index("gr"), lax.axis_index("gc")
    z, c = d // 2, d % 2
    other = 1 - c
    gy, gx = g // 2, g % 2
    pos = (1 - gx) * gy + gx * (G - 1 - gy)
    ry, rx = z // 2, z % 2
    turn = (pos - ((1 - rx) * ry + rx * (G - 1 - ry)) + G) % G
    is_root = turn == 0

    def ring_device(at):
        at = at % G
        far = at // (G // 2)
        return (1 - far) * 2 * at + far * (2 * (G - 1 - at) + 1)

    ahead, behind = ring_device(pos + 1), ring_device(pos + G - 1)
    send_way = (1 - c) * ahead + c * behind
    not_first, not_last = z > 0, z < Z - 1

    barrier = pltpu.get_barrier_semaphore()

    def greet(device):
        pl.semaphore_signal(barrier, inc=1, device_id=device, device_id_type=MESH)

    greet((g, 2 * z + other))
    for core in range(2):
        greet((ahead, 2 * z + core))
        greet((behind, 2 * z + core))

    @pl.when(not_last)
    def _():
        greet((g, d + 2))

    @pl.when(not_first)
    def _():
        greet((g, d - 2))

    tail = pl.ds(pixels, extra)
    left[d, pl.ds(pixels, half)] = data_ref[0]
    left[d, pl.ds(pixels + half, half)] = data_ref[1]

    pl.semaphore_wait(barrier, 5 + not_last.astype(jnp.int32) + not_first.astype(jnp.int32))

    def remote(src, dst, send_sem, recv_sem, device):
        return pltpu.make_async_remote_copy(
            src_ref=src, dst_ref=dst, send_sem=send_sem, recv_sem=recv_sem, device_id=device, device_id_type=MESH
        )

    def arrived(piece, sem):
        remote(piece, piece, twin_sem.at[0], sem, (g, d)).wait_recv()

    def spread(piece, zb, sem):
        @pl.when((zb <= z) & not_last)
        def _():
            remote(piece, piece, up_sem.at[zb], sem, (g, d + 2)).start()

        @pl.when((zb >= z) & not_first)
        def _():
            remote(piece, piece, down_sem.at[zb], sem, (g, d - 2)).start()

        remote(piece, piece, twin_sem.at[zb], sem, (g, 2 * z + other)).start()

    def start_of(m):
        return pl.multiple_of((m % 2) * Q + (m // 2) * rows, rows)

    def broadcast(piece, zb, block, m):
        at = pl.multiple_of((m // 2) * rows, rows)
        remote(
            piece, right.at[block, pl.ds(at, rows)], root_sem.at[zb], got_right.at[block, m // 2],
            (send_way, 2 * z + m % 2),
        ).start()

    def weights():
        table = jnp.transpose(table_ref[...])
        first = table.astype(jnp.bfloat16)
        rest = table - first.astype(jnp.float32)
        second = rest.astype(jnp.bfloat16)
        third = (rest - second.astype(jnp.float32)).astype(jnp.bfloat16)
        lanes, lines = table.shape
        for b in range(C):
            ids = ids_ref[pl.ds(b, 1)]
            line = lax.broadcasted_iota(jnp.int32, (lines, width), 0)
            pick = (line == ids // lanes).astype(jnp.float32).astype(jnp.bfloat16)
            near = sum(jnp.dot(t, pick, preferred_element_type=jnp.float32) for t in (first, second, third))
            lane = lax.broadcasted_iota(jnp.int32, (lanes, width), 0)
            scale[pl.ds(b, 1)] = jnp.sum(jnp.where(lane == ids % lanes, near, 0.0), axis=0, keepdims=True)

    def scaled(value, b):
        return value.astype(jnp.float32) * scale[pl.ds(b, 1)]

    def prepare(i):
        here = pl.ds(i * rows, rows)

        @pl.when(is_root)
        def _():
            for b in range(C):
                value = scaled(left[b, pl.ds(pl.multiple_of(c * Q + i * rows, rows), rows)], b)
                weighted[b * width:(b + 1) * width, here] = jnp.transpose(value).astype(jnp.bfloat16)

        @pl.when(turn > 0)
        def _():
            for b in range(C):
                value = scaled(right[b, here], b)
                weighted[b * width:(b + 1) * width, here] = jnp.transpose(value).astype(jnp.bfloat16)

    def tile(m, i):
        cut = pl.ds(start_of(m), rows)
        lines = jnp.concatenate([left[b, cut] for b in range(C)], axis=1)
        here = pl.ds(i * rows, rows)
        fisher[cut, here] = jnp.dot(lines, weighted[:, here], preferred_element_type=jnp.float32)

    spread(left.at[d, tail], z, got.at[d, S])
    late = Z + G - 2

    def step(s, carry):
        @pl.when(s < S)
        def _():
            at = start_of(s)
            cut = pl.ds(at, rows)
            value = phase_ref[:, :, cut].reshape(width, rows).astype(jnp.float32)
            left[d, cut] = jnp.transpose(value).astype(jnp.bfloat16)
            spread(left.at[d, cut], z, got.at[d, s])

            @pl.when(is_root)
            def _():
                broadcast(left.at[d, cut], z, d, s)

        for zb in range(Z):
            away = jnp.maximum(zb - z, z - zb)
            mine, twin = 2 * zb + c, 2 * zb + other
            m = s - away

            @pl.when((zb != z) & (m >= 0) & (m < S))
            def _():
                piece = left.at[mine, pl.ds(start_of(m), rows)]
                arrived(piece, got.at[mine, m])
                spread(piece, zb, got.at[mine, m])

                @pl.when(is_root)
                def _():
                    broadcast(piece, zb, mine, m)

            @pl.when((zb != z) & (s == away))
            def _():
                piece = left.at[mine, tail]
                arrived(piece, got.at[mine, S])
                spread(piece, zb, got.at[mine, S])

            n = s - away - 1

            @pl.when((n >= 0) & (n < S))
            def _():
                arrived(left.at[twin, pl.ds(start_of(n), rows)], got.at[twin, n])

            for e in range(2):
                hops = turn if e == 0 else G - turn
                r = s - away - hops

                @pl.when((turn > 0) & (r >= 0) & (r < S) & (r % 2 == c))
                def _():
                    block = 2 * zb + e
                    piece = right.at[block, pl.ds(pl.multiple_of((r // 2) * rows, rows), rows)]
                    arrived(piece, got_right.at[block, r // 2])

                    @pl.when(hops < G - 1)
                    def _():
                        remote(
                            piece, piece, ring_sem.at[block], got_right.at[block, r // 2],
                            (ahead if e == 0 else behind, d),
                        ).start()

        @pl.when(s == 1)
        def _():
            weights()

        for i in range(parts):
            ripe = 2 * i + c + late

            @pl.when(s == ripe)
            def _():
                prepare(i)
                lax.fori_loop(0, jnp.minimum(s - Z, S), lambda m, _: (tile(m, i), 0)[1], 0)

            @pl.when((s >= ripe) & (s >= Z) & (s - Z < S))
            def _():
                tile(s - Z, i)

        @pl.when(s == S + Z - 1)
        def _():
            for zb in range(Z):
                twin = 2 * zb + other
                arrived(left.at[twin, tail], got.at[twin, S])
            skip = d * owned % 16
            cut = pl.ds(pl.multiple_of(d * owned - skip, 16), spare.shape[0])
            mine = jnp.concatenate([scaled(left[b, cut], b).astype(jnp.bfloat16) for b in range(C)], axis=1)
            columns = jnp.concatenate([left[b, tail] for b in range(C)], axis=0)
            spare[...] = jnp.dot(mine, columns, preferred_element_type=jnp.float32)
            maps[...] = spare[pl.ds(pl.multiple_of(skip, 8), owned)]

        return carry

    lax.fori_loop(0, S + late, step, 0)

    def sent(piece, sem):
        remote(piece, piece, sem, got.at[0, 0], (g, d)).wait_send()

    for zb in range(Z):
        mine = 2 * zb + c
        sent(left.at[mine], twin_sem.at[zb])

        @pl.when((zb <= z) & not_last)
        def _():
            sent(left.at[mine], up_sem.at[zb])

        @pl.when((zb >= z) & not_first)
        def _():
            sent(left.at[mine], down_sem.at[zb])

        @pl.when(is_root)
        def _():
            sent(left.at[mine, pl.ds(0, pixels)], root_sem.at[zb])

        for e in range(2):
            block = 2 * zb + e
            hops = turn if e == 0 else G - turn

            @pl.when((turn > 0) & (hops < G - 1))
            def _():
                sent(right.at[block], ring_sem.at[block])


def shards(phase, data, column_ids, noise_weight):
    G, C = lax.axis_size("gr"), lax.axis_size("gc")
    _, pixels, half = phase.shape
    width = 2 * half
    Q = pixels * G // C
    owned = pixels // C
    rows = math.gcd(Q, 256)
    lanes = 128
    tall = owned if owned % 16 == 0 else (owned + 8 + 15) // 16 * 16
    ids = column_ids.reshape(C, half)
    ids = jnp.concatenate([ids, ids], axis=1)
    table = noise_weight.reshape(-1, lanes)
    dma = pltpu.SemaphoreType.DMA
    Z = C // 2
    return pl.pallas_call(
        functools.partial(sky_kernel, G, C, rows),
        out_shape=(
            pltpu.VMEM((pixels, Q), jnp.float32),
            pltpu.VMEM((owned, data.shape[2]), jnp.float32),
        ),
        in_specs=[pl.BlockSpec(memory_space=pltpu.VMEM)] * 4,
        out_specs=(pl.BlockSpec(memory_space=pltpu.VMEM),) * 2,
        scratch_shapes=[
            pltpu.VMEM((C, pixels + width, width), jnp.bfloat16),
            pltpu.VMEM((C, Q, width), jnp.bfloat16),
            pltpu.VMEM((C * width, Q), jnp.bfloat16),
            pltpu.VMEM((C, width), jnp.float32),
            pltpu.VMEM((tall, data.shape[2]), jnp.float32),
            dma((Z,)), dma((Z,)), dma((Z,)), dma((Z,)), dma((C,)),
            dma((C, 2 * (Q // rows) + 1)), dma((C, Q // rows)),
        ],
        compiler_params=pltpu.CompilerParams(
            collective_id=0, has_side_effects=True, vmem_limit_bytes=24 * 2**20
        ),
    )(jnp.transpose(phase, (0, 2, 1)), data, ids, table)


def solution(mesh):
    return jax.shard_map(
        shards,
        mesh=mesh,
        in_specs=(P(None, "gr", "gc"), P(None, "gc", None), P(), P()),
        out_specs=(P("gr", "gc"), P(("gr", "gc"), None)),
        check_vma=False,
    )
```

time: 101 us -> 89.7 us (0.89)
  Pallas kernels: 92.6 us -> 77.5 us
  local copies, waits for them, and re-layouts: 5.8 us -> 10.9 us
  other arithmetic: 1.46 us -> 0.08 us
    pallas_call x2 -> x1, Pallas kernels: 92.6 us -> 77.5 us  [shards(): pl.pallas_call(functools.partial(sky_kernel, G, C, rows), out_shape=(pltp...]
    unnamed x5 -> x8, local copies, waits for them, and re-layouts: 2.59 us -> 10.2 us
    gather x1 -> x0, local copies, waits for them, and re-layouts: 3.13 us -> none  [shards(): weight = jnp.take(noise_weight, column_ids).reshape(C, 1, half)]
    select_n x2 -> x0, other arithmetic: 1.38 us -> none  [shards(): weight = jnp.take(noise_weight, column_ids).reshape(C, 1, half)]
where the time goes in v2:
time: 89.7 us; the launch traced here: 89.2 us
  Pallas kernels  77.5 us (86%)
  local copies, waits for them, and re-layouts  10.9 us (12%)
    pallas_call x1, Pallas kernels, shards(): pl.pallas_call(functools.partial(sky_kernel, G, C, rows), out_shape=(pltp...  77.5 us
    unnamed x8, local copies, waits for them, and re-layouts  10.2 us

profile of v2, /device:TPU:3, one launch (start us, length us, event | category | flops | bytes accessed | tf_op | source)
XLA Modules:
  0.0 89.2 jit_solution(8578980083162396122)
XLA Ops:
  0.6 0.8 reshape.10
  1.4 0.1 pad_add_fusion.ids_ref
  1.5 0.0 copy-start
  1.5 1.1 %copy-done = bf16[2,3072,64]{1,2,0:T(8,128)(2,1)S(1)} copy-done((bf16[2,3072,64]{1,2,0:T(8,128)(2,1)S(1)}, bf16[2,3072,64]{1,2,0:T(8,128)(2,1)}, u32[]{:S(2)}) %copy-start) | copy-done | bytes 786456
  2.6 0.0 copy-start.1
  2.6 0.8 copy-done.1
  3.4 0.0 copy-start.2
  3.4 0.8 copy-done.2
  4.1 77.5 %shard_map.59 = (f32[3072,1536]{1,0:T(8,128)S(1)}, f32[384,128]{1,0:T(8,128)S(1)}) custom-call(bf16[2,64,3072]{2,1,0:T(8,128)(2,1)S(1)} %bitcast.2, bf16[2,64,128]{2,1,0:T(8,128)(2,1)S(1)} %copy-done.1, s32[8,128]{1,0:T(8,128)S(1)} %pad_add_fusion.ids_ref, f32[64,128]{1,0:T(8,128)S(1)} %bitcast.3), custom_call_target="tpu_custom_call" | custom-call | tf_op jit(solution)/shard_map/pallas_call | solution.py:270
  81.6 6.9 %copy.8 = f32[3072,1536]{1,0:T(8,128)} copy(f32[3072,1536]{1,0:T(8,128)S(1)} %get-tuple-element.2) | data formatting | bytes 37748736
  88.5 0.7 copy.9
Async XLA Ops:
  1.5 1.1 %copy-start = (bf16[2,3072,64]{1,2,0:T(8,128)(2,1)S(1)}, bf16[2,3072,64]{1,2,0:T(8,128)(2,1)}, u32[]{:S(2)}) copy-start(bf16[2,3072,64]{1,2,0:T(8,128)(2,1)} %param.4) | copy-start | bytes 2359300
  2.6 0.8 copy-start.1
  3.4 0.8 copy-start.2

commit v3 on v2

--- a/solution.py
+++ b/solution.py
@@ -9,11 +9,14 @@
 from jax.sharding import PartitionSpec as P
 
 MESH = pl.DeviceIdType.MESH
+ROWS = 128
+VMEM_BYTES = 64 * 2**20
+SPARE_BYTES = 64 * 2**10
 
 
 def sky_kernel(
-    G, C, rows, phase_ref, data_ref, ids_ref, table_ref, fisher, maps, left, right, weighted, scale, spare,
-    up_sem, down_sem, twin_sem, root_sem, ring_sem, got, got_right,
+    G, C, rows, group, phase_in, data_in, ids_in, table_in, fisher, maps, phase_ref, data_ref, ids_ref, table_ref,
+    left, right, weighted, scale, spare, in_sem, up_sem, down_sem, twin_sem, root_sem, ring_sem, got, got_right,
 ):
     Z = C // 2
     half, pixels = phase_ref.shape[1:]
@@ -41,6 +44,15 @@
     send_way = (1 - c) * ahead + c * behind
     not_first, not_last = z > 0, z < Z - 1
 
+    incoming = [
+        pltpu.make_async_copy(src, dst, in_sem.at[k])
+        for k, (src, dst) in enumerate(
+            ((data_in, data_ref), (phase_in, phase_ref), (ids_in, ids_ref), (table_in, table_ref))
+        )
+    ]
+    for copy in incoming:
+        copy.start()
+
     barrier = pltpu.get_barrier_semaphore()
 
     def greet(device):
@@ -60,6 +72,7 @@
         greet((g, d - 2))
 
     tail = pl.ds(pixels, extra)
+    incoming[0].wait()
     left[d, pl.ds(pixels, half)] = data_ref[0]
     left[d, pl.ds(pixels + half, half)] = data_ref[1]
 
@@ -101,24 +114,34 @@
         second = rest.astype(jnp.bfloat16)
         third = (rest - second.astype(jnp.float32)).astype(jnp.bfloat16)
         lanes, lines = table.shape
-        for b in range(C):
-            ids = ids_ref[pl.ds(b, 1)]
+        for b in range(0, C, 2):
+            ids = ids_ref[pl.ds(b // 2, 1)]
             line = lax.broadcasted_iota(jnp.int32, (lines, width), 0)
             pick = (line == ids // lanes).astype(jnp.float32).astype(jnp.bfloat16)
             near = sum(jnp.dot(t, pick, preferred_element_type=jnp.float32) for t in (first, second, third))
             lane = lax.broadcasted_iota(jnp.int32, (lanes, width), 0)
-            scale[pl.ds(b, 1)] = jnp.sum(jnp.where(lane == ids % lanes, near, 0.0), axis=0, keepdims=True)
+            both = jnp.sum(jnp.where(lane == ids % lanes, near, 0.0), axis=0, keepdims=True)
+            turned = jnp.concatenate([both[:, half:], both[:, :half]], axis=1)
+            low = lax.broadcasted_iota(jnp.int32, (1, width), 1) < half
+            scale[pl.ds(b, 1)] = jnp.where(low, both, turned)
+            scale[pl.ds(b + 1, 1)] = jnp.where(low, turned, both)
 
     def scaled(value, b):
         return value.astype(jnp.float32) * scale[pl.ds(b, 1)]
 
+    wide = group * rows
+    units = parts // group
+
+    def unit_start(u):
+        return pl.multiple_of((u % 2) * Q + (u // 2) * wide, wide)
+
     def prepare(i):
-        here = pl.ds(i * rows, rows)
+        here = pl.ds(i * wide, wide)
 
         @pl.when(is_root)
         def _():
             for b in range(C):
-                value = scaled(left[b, pl.ds(pl.multiple_of(c * Q + i * rows, rows), rows)], b)
+                value = scaled(left[b, pl.ds(pl.multiple_of(c * Q + i * wide, wide), wide)], b)
                 weighted[b * width:(b + 1) * width, here] = jnp.transpose(value).astype(jnp.bfloat16)
 
         @pl.when(turn > 0)
@@ -127,13 +150,15 @@
                 value = scaled(right[b, here], b)
                 weighted[b * width:(b + 1) * width, here] = jnp.transpose(value).astype(jnp.bfloat16)
 
-    def tile(m, i):
-        cut = pl.ds(start_of(m), rows)
+    def tile(u, i):
+        cut = pl.ds(unit_start(u), wide)
         lines = jnp.concatenate([left[b, cut] for b in range(C)], axis=1)
-        here = pl.ds(i * rows, rows)
+        here = pl.ds(i * wide, wide)
         fisher[cut, here] = jnp.dot(lines, weighted[:, here], preferred_element_type=jnp.float32)
 
     spread(left.at[d, tail], z, got.at[d, S])
+    for copy in incoming[1:]:
+        copy.wait()
     late = Z + G - 2
 
     def step(s, carry):
@@ -197,17 +222,21 @@
         def _():
             weights()
 
-        for i in range(parts):
-            ripe = 2 * i + c + late
+        last = s - Z - 2 * (group - 1)
+        cycle = last % (2 * group)
+        unit = last // (2 * group) * 2 + cycle
+        done = jnp.minimum(last // (2 * group) * 2 + jnp.minimum(cycle, 2), 2 * units)
+        for i in range(units):
+            ripe = 2 * (group * i + group - 1) + c + late
 
             @pl.when(s == ripe)
             def _():
                 prepare(i)
-                lax.fori_loop(0, jnp.minimum(s - Z, S), lambda m, _: (tile(m, i), 0)[1], 0)
-
-            @pl.when((s >= ripe) & (s >= Z) & (s - Z < S))
-            def _():
-                tile(s - Z, i)
+                lax.fori_loop(0, done, lambda u, _: (tile(u, i), 0)[1], 0)
+
+            @pl.when((s >= ripe) & (last >= 0) & (cycle < 2) & (unit < 2 * units))
+            def _():
+                tile(unit, i)
 
         @pl.when(s == S + Z - 1)
         def _():
@@ -259,33 +288,37 @@
     width = 2 * half
     Q = pixels * G // C
     owned = pixels // C
-    rows = math.gcd(Q, 256)
+    wide = math.gcd(Q, 256)
+    rows = math.gcd(wide, ROWS)
     lanes = 128
     tall = owned if owned % 16 == 0 else (owned + 8 + 15) // 16 * 16
-    ids = column_ids.reshape(C, half)
-    ids = jnp.concatenate([ids, ids], axis=1)
+    ids = column_ids.reshape(C // 2, width)
     table = noise_weight.reshape(-1, lanes)
     dma = pltpu.SemaphoreType.DMA
     Z = C // 2
     return pl.pallas_call(
-        functools.partial(sky_kernel, G, C, rows),
+        functools.partial(sky_kernel, G, C, rows, wide // rows),
         out_shape=(
             pltpu.VMEM((pixels, Q), jnp.float32),
             pltpu.VMEM((owned, data.shape[2]), jnp.float32),
         ),
-        in_specs=[pl.BlockSpec(memory_space=pltpu.VMEM)] * 4,
+        in_specs=[pl.BlockSpec(memory_space=pltpu.HBM)] * 4,
         out_specs=(pl.BlockSpec(memory_space=pltpu.VMEM),) * 2,
         scratch_shapes=[
+            pltpu.VMEM((2, half, pixels), jnp.bfloat16),
+            pltpu.VMEM(data.shape, jnp.bfloat16),
+            pltpu.VMEM(ids.shape, jnp.int32),
+            pltpu.VMEM(table.shape, jnp.float32),
             pltpu.VMEM((C, pixels + width, width), jnp.bfloat16),
             pltpu.VMEM((C, Q, width), jnp.bfloat16),
             pltpu.VMEM((C * width, Q), jnp.bfloat16),
             pltpu.VMEM((C, width), jnp.float32),
             pltpu.VMEM((tall, data.shape[2]), jnp.float32),
-            dma((Z,)), dma((Z,)), dma((Z,)), dma((Z,)), dma((C,)),
+            dma((4,)), dma((Z,)), dma((Z,)), dma((Z,)), dma((Z,)), dma((C,)),
             dma((C, 2 * (Q // rows) + 1)), dma((C, Q // rows)),
         ],
         compiler_params=pltpu.CompilerParams(
-            collective_id=0, has_side_effects=True, vmem_limit_bytes=24 * 2**20
+            collective_id=0, has_side_effects=True, vmem_limit_bytes=VMEM_BYTES - 4 * (pixels * Q + owned * data.shape[2]) - SPARE_BYTES
         ),
     )(jnp.transpose(phase, (0, 2, 1)), data, ids, table)
 

time: 89.7 us -> 104 us (1.16)
  Pallas kernels: 77.5 us -> 95.9 us
  local copies, waits for them, and re-layouts: 10.9 us -> 7.53 us
    pallas_call x1, Pallas kernels: 77.5 us -> 95.9 us  [shards(): pl.pallas_call(functools.partial(sky_kernel, G, C, rows, wide // rows), o...]
    unnamed x8 -> x2, local copies, waits for them, and re-layouts: 10.2 us -> 7.53 us
where the time goes in v3:
time: 104 us
  Pallas kernels  95.9 us (92%)
  local copies, waits for them, and re-layouts  7.53 us (7%)
    pallas_call x1, Pallas kernels, shards(): pl.pallas_call(functools.partial(sky_kernel, G, C, rows, wide // rows), o...  95.9 us
    unnamed x2, local copies, waits for them, and re-layouts  7.53 us

profile of v3, /device:TPU:3, one launch (start us, length us, event | category | flops | bytes accessed | tf_op | source)
XLA Modules:
  0.0 104.0 jit_solution(357674235307323763)
XLA Ops:
  0.6 95.9 %shard_map.59 = (f32[3072,1536]{1,0:T(8,128)S(1)}, f32[384,128]{1,0:T(8,128)S(1)}) custom-call(bf16[2,64,3072]{2,1,0:T(8,128)(2,1)} %bitcast.3, bf16[2,64,128]{2,1,0:T(8,128)(2,1)} %data_in.1, s32[4,128]{1,0:T(4,128)} %bitcast.5, f32[64,128]{1,0:T(8,128)} %bitcast.4), custom_call_target="tpu_custom_call" | custom-call | tf_op jit(solution)/shard_map/pallas_call | solution.py:299
  96.5 6.9 %copy.8 = f32[3072,1536]{1,0:T(8,128)} copy(f32[3072,1536]{1,0:T(8,128)S(1)} %get-tuple-element.2) | data formatting | bytes 37748736
  103.4 0.7 copy.9

commit v4 on v3

--- a/solution.py
+++ b/solution.py
@@ -9,21 +9,21 @@
 from jax.sharding import PartitionSpec as P
 
 MESH = pl.DeviceIdType.MESH
-ROWS = 128
+ROWS = 256
+LATE = 2
 VMEM_BYTES = 64 * 2**20
 SPARE_BYTES = 64 * 2**10
 
 
 def sky_kernel(
-    G, C, rows, group, phase_in, data_in, ids_in, table_in, fisher, maps, phase_ref, data_ref, ids_ref, table_ref,
-    left, right, weighted, scale, spare, in_sem, up_sem, down_sem, twin_sem, root_sem, ring_sem, got, got_right,
+    G, C, rows, group, phase_in, data_in, ids_in, table_in, fisher, left, weighted, scale,
+    phase_ref, data_ref, ids_ref, table_ref, right, in_sem, up_sem, down_sem, twin_sem, root_sem, ring_sem, got, got_right,
 ):
     Z = C // 2
     half, pixels = phase_ref.shape[1:]
     width = 2 * half
     extra = data_ref.shape[0] * data_ref.shape[1]
     Q = right.shape[1]
-    owned = pixels // C
     parts = Q // rows
     S = 2 * parts
     g, d = lax.axis_index("gr"), lax.axis_index("gc")
@@ -131,6 +131,7 @@
 
     wide = group * rows
     units = parts // group
+    early = fisher.shape[1] // wide
 
     def unit_start(u):
         return pl.multiple_of((u % 2) * Q + (u // 2) * wide, wide)
@@ -232,7 +233,11 @@
             @pl.when(s == ripe)
             def _():
                 prepare(i)
-                lax.fori_loop(0, done, lambda u, _: (tile(u, i), 0)[1], 0)
+                if i < early:
+                    lax.fori_loop(0, done, lambda u, _: (tile(u, i), 0)[1], 0)
+
+            if i >= early:
+                continue
 
             @pl.when((s >= ripe) & (last >= 0) & (cycle < 2) & (unit < 2 * units))
             def _():
@@ -243,12 +248,6 @@
             for zb in range(Z):
                 twin = 2 * zb + other
                 arrived(left.at[twin, tail], got.at[twin, S])
-            skip = d * owned % 16
-            cut = pl.ds(pl.multiple_of(d * owned - skip, 16), spare.shape[0])
-            mine = jnp.concatenate([scaled(left[b, cut], b).astype(jnp.bfloat16) for b in range(C)], axis=1)
-            columns = jnp.concatenate([left[b, tail] for b in range(C)], axis=0)
-            spare[...] = jnp.dot(mine, columns, preferred_element_type=jnp.float32)
-            maps[...] = spare[pl.ds(pl.multiple_of(skip, 8), owned)]
 
         return carry
 
@@ -280,6 +279,40 @@
             @pl.when((turn > 0) & (hops < G - 1))
             def _():
                 sent(right.at[block], ring_sem.at[block])
+
+
+def finish_kernel(C, owned, fisher, left, weighted, scale, out, maps, columns, mine, out_sem, late_sem, maps_sem):
+    pixels, early = fisher.shape
+    width = left.shape[2]
+    step = math.gcd(pixels, 512)
+    late = columns.shape[1]
+    copy = pltpu.make_async_copy(fisher, out.at[:, pl.ds(0, early)], out_sem)
+    copy.start()
+
+    skip = lax.axis_index("gc") * owned % 16
+    cut = pl.ds(pl.multiple_of(lax.axis_index("gc") * owned - skip, 16), mine.shape[0])
+    rows = [(left[b, cut].astype(jnp.float32) * scale[pl.ds(b, 1)]).astype(jnp.bfloat16) for b in range(C)]
+    data = jnp.concatenate([left[b, pl.ds(pixels, width)] for b in range(C)], axis=0)
+    mine[...] = jnp.dot(jnp.concatenate(rows, axis=1), data, preferred_element_type=jnp.float32)
+    kept = pltpu.make_async_copy(mine.at[pl.ds(pl.multiple_of(skip, 8), owned)], maps, maps_sem)
+    kept.start()
+
+    def strip(k):
+        part = pl.ds(pl.multiple_of(k * step, step), step)
+        return part, pltpu.make_async_copy(columns.at[part], out.at[part, pl.ds(early, late)], late_sem.at[k])
+
+    def multiply(k, carry):
+        part, send = strip(k)
+        lines = jnp.concatenate([left[b, part] for b in range(C)], axis=1)
+        columns[part] = jnp.dot(lines, weighted[:, early:], preferred_element_type=jnp.float32)
+        send.start()
+        return carry
+
+    lax.fori_loop(0, pixels // step, multiply, 0)
+    for k in range(pixels // step):
+        strip(k)[1].wait()
+    kept.wait()
+    copy.wait()
 
 
 def shards(phase, data, column_ids, noise_weight):
@@ -290,37 +323,53 @@
     owned = pixels // C
     wide = math.gcd(Q, 256)
     rows = math.gcd(wide, ROWS)
+    late = LATE * wide
     lanes = 128
     tall = owned if owned % 16 == 0 else (owned + 8 + 15) // 16 * 16
     ids = column_ids.reshape(C // 2, width)
     table = noise_weight.reshape(-1, lanes)
     dma = pltpu.SemaphoreType.DMA
     Z = C // 2
-    return pl.pallas_call(
+    held = (
+        ((pixels, Q - late), jnp.float32),
+        ((C, pixels + width, width), jnp.bfloat16),
+        ((C * width, Q), jnp.bfloat16),
+        ((C, width), jnp.float32),
+    )
+    held_bytes = sum(math.prod(shape) * jnp.dtype(kind).itemsize for shape, kind in held)
+    kept = pl.pallas_call(
         functools.partial(sky_kernel, G, C, rows, wide // rows),
-        out_shape=(
-            pltpu.VMEM((pixels, Q), jnp.float32),
-            pltpu.VMEM((owned, data.shape[2]), jnp.float32),
-        ),
+        out_shape=tuple(pltpu.VMEM(shape, kind) for shape, kind in held),
         in_specs=[pl.BlockSpec(memory_space=pltpu.HBM)] * 4,
-        out_specs=(pl.BlockSpec(memory_space=pltpu.VMEM),) * 2,
+        out_specs=(pl.BlockSpec(memory_space=pltpu.VMEM),) * 4,
         scratch_shapes=[
             pltpu.VMEM((2, half, pixels), jnp.bfloat16),
             pltpu.VMEM(data.shape, jnp.bfloat16),
             pltpu.VMEM(ids.shape, jnp.int32),
             pltpu.VMEM(table.shape, jnp.float32),
-            pltpu.VMEM((C, pixels + width, width), jnp.bfloat16),
             pltpu.VMEM((C, Q, width), jnp.bfloat16),
-            pltpu.VMEM((C * width, Q), jnp.bfloat16),
-            pltpu.VMEM((C, width), jnp.float32),
-            pltpu.VMEM((tall, data.shape[2]), jnp.float32),
             dma((4,)), dma((Z,)), dma((Z,)), dma((Z,)), dma((Z,)), dma((C,)),
             dma((C, 2 * (Q // rows) + 1)), dma((C, Q // rows)),
         ],
         compiler_params=pltpu.CompilerParams(
-            collective_id=0, has_side_effects=True, vmem_limit_bytes=VMEM_BYTES - 4 * (pixels * Q + owned * data.shape[2]) - SPARE_BYTES
+            collective_id=0, has_side_effects=True, vmem_limit_bytes=VMEM_BYTES - held_bytes - SPARE_BYTES
         ),
     )(jnp.transpose(phase, (0, 2, 1)), data, ids, table)
+    return pl.pallas_call(
+        functools.partial(finish_kernel, C, owned),
+        out_shape=(
+            jax.ShapeDtypeStruct((pixels, Q), jnp.float32),
+            jax.ShapeDtypeStruct((owned, data.shape[2]), jnp.float32),
+        ),
+        in_specs=[pl.BlockSpec(memory_space=pltpu.VMEM)] * 4,
+        out_specs=(pl.BlockSpec(memory_space=pltpu.HBM),) * 2,
+        scratch_shapes=[
+            pltpu.VMEM((pixels, late), jnp.float32),
+            pltpu.VMEM((tall, data.shape[2]), jnp.float32),
+            dma, dma((pixels // math.gcd(pixels, 512),)), dma,
+        ],
+        compiler_params=pltpu.CompilerParams(vmem_limit_bytes=12 * 2**20),
+    )(*(pltpu.with_memory_space_constraint(array, pltpu.VMEM) for array in kept))
 
 
 def solution(mesh):

time: 104 us -> 79.6 us (0.77); the launches traced: 104 us -> 78.5 us
  Pallas kernels: 95.9 us -> 77.8 us
  local copies, waits for them, and re-layouts: 7.53 us -> 0 us
    pallas_call x1, Pallas kernels: 95.9 us -> 71 us  [shards(): pl.pallas_call(functools.partial(sky_kernel, G, C, rows, wide // rows), o...]
    unnamed x2 -> x0, local copies, waits for them, and re-layouts: 7.53 us -> none
    pallas_call x0 -> x1, Pallas kernels: none -> 6.83 us  [shards(): pl.pallas_call(functools.partial(finish_kernel, C, owned), out_shape=(jax...]
where the time goes in v4:
time: 79.6 us; the launch traced here: 78.5 us
  Pallas kernels  77.8 us (98%)
    pallas_call x1, Pallas kernels, shards(): pl.pallas_call(functools.partial(sky_kernel, G, C, rows, wide // rows), o...  71 us
    pallas_call x1, Pallas kernels, shards(): pl.pallas_call(functools.partial(finish_kernel, C, owned), out_shape=(jax...  6.83 us

profile of v4, /device:TPU:3, one launch (start us, length us, event | category | flops | bytes accessed | tf_op | source)
XLA Modules:
  0.0 78.5 jit_solution(17886320421647960710)
XLA Ops:
  0.6 71.0 %shard_map.59 = (f32[3072,1024]{1,0:T(8,128)S(1)}, bf16[8,3200,128]{2,1,0:T(8,128)(2,1)S(1)}, bf16[1024,1536]{1,0:T(8,128)(2,1)S(1)}, f32[8,128]{1,0:T(8,128)S(1)}) custom-call(bf16[2,64,3072]{2,1,0:T(8,128)(2,1)} %bitcast.3, bf16[2,64,128]{2,1,0:T(8,128)(2,1)} %data_in.1, s32[4,128]{1,0:T(4,128)} %bitcast.5, f32[64,128]{1,0:T(8,128)} %bitcast.4), custom_call_target="tpu_custom_call" | custom-call | tf_op jit(solution)/shard_map/pallas_call | solution.py:340
  71.6 6.8 %shard_map.60 = (f32[3072,1536]{1,0:T(8,128)}, f32[384,128]{1,0:T(8,128)}) custom-call(f32[3072,1024]{1,0:T(8,128)S(1)} %get-tuple-element.6.fisher, bf16[8,3200,128]{2,1,0:T(8,128)(2,1)S(1)} %get-tuple-element.7.left, bf16[1024,1536]{1,0:T(8,128)(2,1)S(1)} %get-tuple-element.8.weighted, f32[8,128]{1,0:T(8,128)S(1)} %get-tuple-element.9.scale), custom_call_target="tpu_custom_call" | custom-call | tf_op jit(solution)/shard_map/pallas_call | solution.py:358

commit v5 on v4

--- a/solution.py
+++ b/solution.py
@@ -10,14 +10,14 @@
 
 MESH = pl.DeviceIdType.MESH
 ROWS = 256
-LATE = 2
+LATE = 3
 VMEM_BYTES = 64 * 2**20
 SPARE_BYTES = 64 * 2**10
 
 
 def sky_kernel(
     G, C, rows, group, phase_in, data_in, ids_in, table_in, fisher, left, weighted, scale,
-    phase_ref, data_ref, ids_ref, table_ref, right, in_sem, up_sem, down_sem, twin_sem, root_sem, ring_sem, got, got_right,
+    phase_ref, data_ref, ids_ref, table_ref, right, in_sem, up_sem, down_sem, twin_sem, root_sem, both_sem, ring_sem, got, got_right,
 ):
     Z = C // 2
     half, pixels = phase_ref.shape[1:]
@@ -42,6 +42,7 @@
 
     ahead, behind = ring_device(pos + 1), ring_device(pos + G - 1)
     send_way = (1 - c) * ahead + c * behind
+    other_way = c * ahead + (1 - c) * behind
     not_first, not_last = z > 0, z < Z - 1
 
     incoming = [
@@ -106,6 +107,13 @@
             piece, right.at[block, pl.ds(at, rows)], root_sem.at[zb], got_right.at[block, m // 2],
             (send_way, 2 * z + m % 2),
         ).start()
+
+        @pl.when(m >= S - 2)
+        def _():
+            remote(
+                piece, right.at[block, pl.ds(at, rows)], both_sem.at[zb], got_right.at[block, m // 2],
+                (other_way, 2 * z + m % 2),
+            ).start()
 
     def weights():
         table = jnp.transpose(table_ref[...])
@@ -204,21 +212,31 @@
 
             for e in range(2):
                 hops = turn if e == 0 else G - turn
-                r = s - away - hops
-
-                @pl.when((turn > 0) & (r >= 0) & (r < S) & (r % 2 == c))
-                def _():
-                    block = 2 * zb + e
+                block = 2 * zb + e
+
+                def take(r, onward):
                     piece = right.at[block, pl.ds(pl.multiple_of((r // 2) * rows, rows), rows)]
                     arrived(piece, got_right.at[block, r // 2])
 
-                    @pl.when(hops < G - 1)
+                    @pl.when(onward)
                     def _():
                         remote(
                             piece, piece, ring_sem.at[block], got_right.at[block, r // 2],
                             (ahead if e == 0 else behind, d),
                         ).start()
 
+                r = s - away - hops
+
+                @pl.when((turn > 0) & (r >= 0) & (r < S - 2) & (r % 2 == c))
+                def _():
+                    take(r, hops < G - 1)
+
+                n = s - away - hops + (G - 2) * (hops // (G - 1))
+
+                @pl.when((turn > 0) & (n >= S - 2) & (n < S) & (n % 2 == c))
+                def _():
+                    take(n, hops < G - 2)
+
         @pl.when(s == 1)
         def _():
             weights()
@@ -228,7 +246,7 @@
         unit = last // (2 * group) * 2 + cycle
         done = jnp.minimum(last // (2 * group) * 2 + jnp.minimum(cycle, 2), 2 * units)
         for i in range(units):
-            ripe = 2 * (group * i + group - 1) + c + late
+            ripe = 2 * (group * i + group - 1) + c + late - (i == units - 1)
 
             @pl.when(s == ripe)
             def _():
@@ -251,7 +269,7 @@
 
         return carry
 
-    lax.fori_loop(0, S + late, step, 0)
+    lax.fori_loop(0, S + late - 1, step, 0)
 
     def sent(piece, sem):
         remote(piece, piece, sem, got.at[0, 0], (g, d)).wait_send()
@@ -271,14 +289,19 @@
         @pl.when(is_root)
         def _():
             sent(left.at[mine, pl.ds(0, pixels)], root_sem.at[zb])
+            sent(left.at[mine, pl.ds(0, 2 * rows)], both_sem.at[zb])
 
         for e in range(2):
             block = 2 * zb + e
             hops = turn if e == 0 else G - turn
 
-            @pl.when((turn > 0) & (hops < G - 1))
+            @pl.when((turn > 0) & (hops < G - 2))
             def _():
                 sent(right.at[block], ring_sem.at[block])
+
+            @pl.when((turn > 0) & (hops == G - 2))
+            def _():
+                sent(right.at[block, pl.ds(0, Q - rows)], ring_sem.at[block])
 
 
 def finish_kernel(C, owned, fisher, left, weighted, scale, out, maps, columns, mine, out_sem, late_sem, maps_sem):
@@ -323,7 +346,7 @@
     owned = pixels // C
     wide = math.gcd(Q, 256)
     rows = math.gcd(wide, ROWS)
-    late = LATE * wide
+    late = min(LATE, Q // wide - 1) * wide
     lanes = 128
     tall = owned if owned % 16 == 0 else (owned + 8 + 15) // 16 * 16
     ids = column_ids.reshape(C // 2, width)
@@ -348,7 +371,7 @@
             pltpu.VMEM(ids.shape, jnp.int32),
             pltpu.VMEM(table.shape, jnp.float32),
             pltpu.VMEM((C, Q, width), jnp.bfloat16),
-            dma((4,)), dma((Z,)), dma((Z,)), dma((Z,)), dma((Z,)), dma((C,)),
+            dma((4,)), dma((Z,)), dma((Z,)), dma((Z,)), dma((Z,)), dma((Z,)), dma((C,)),
             dma((C, 2 * (Q // rows) + 1)), dma((C, Q // rows)),
         ],
         compiler_params=pltpu.CompilerParams(
@@ -368,7 +391,7 @@
             pltpu.VMEM((tall, data.shape[2]), jnp.float32),
             dma, dma((pixels // math.gcd(pixels, 512),)), dma,
         ],
-        compiler_params=pltpu.CompilerParams(vmem_limit_bytes=12 * 2**20),
+        compiler_params=pltpu.CompilerParams(vmem_limit_bytes=15 * 2**20),
     )(*(pltpu.with_memory_space_constraint(array, pltpu.VMEM) for array in kept))
 
 

time: 79.6 us -> 77.9 us (0.979)
  the two profiles are of different devices: /device:TPU:3 before, /device:TPU:6 now
where the time goes in v5:
time: 77.9 us; the launch traced here: 77.7 us
  Pallas kernels  77.1 us (99%)
    pallas_call x1, Pallas kernels, shards(): pl.pallas_call(functools.partial(sky_kernel, G, C, rows, wide // rows), o...  69.6 us
    pallas_call x1, Pallas kernels, shards(): pl.pallas_call(functools.partial(finish_kernel, C, owned), out_shape=(jax...  7.47 us

profile of v5, /device:TPU:6, one launch (start us, length us, event | category | flops | bytes accessed | tf_op | source)
XLA Modules:
  0.0 77.7 jit_solution(3872033776503420544)
XLA Ops:
  0.6 69.6 %shard_map.59 = (f32[3072,768]{1,0:T(8,128)S(1)}, bf16[8,3200,128]{2,1,0:T(8,128)(2,1)S(1)}, bf16[1024,1536]{1,0:T(8,128)(2,1)S(1)}, f32[8,128]{1,0:T(8,128)S(1)}) custom-call(bf16[2,64,3072]{2,1,0:T(8,128)(2,1)} %bitcast.3, bf16[2,64,128]{2,1,0:T(8,128)(2,1)} %data_in.1, s32[4,128]{1,0:T(4,128)} %bitcast.5, f32[64,128]{1,0:T(8,128)} %bitcast.4), custom_call_target="tpu_custom_call" | custom-call | tf_op jit(solution)/shard_map/pallas_call | solution.py:363
  70.2 7.5 %shard_map.60 = (f32[3072,1536]{1,0:T(8,128)}, f32[384,128]{1,0:T(8,128)}) custom-call(f32[3072,768]{1,0:T(8,128)S(1)} %get-tuple-element.6.fisher, bf16[8,3200,128]{2,1,0:T(8,128)(2,1)S(1)} %get-tuple-element.7.left, bf16[1024,1536]{1,0:T(8,128)(2,1)S(1)} %get-tuple-element.8.weighted, f32[8,128]{1,0:T(8,128)S(1)} %get-tuple-element.9.scale), custom_call_target="tpu_custom_call" | custom-call | tf_op jit(solution)/shard_map/pallas_call | solution.py:381

commit v6 on v5

--- a/solution.py
+++ b/solution.py
@@ -108,7 +108,7 @@
             (send_way, 2 * z + m % 2),
         ).start()
 
-        @pl.when(m >= S - 2)
+        @pl.when(m >= S - 4)
         def _():
             remote(
                 piece, right.at[block, pl.ds(at, rows)], both_sem.at[zb], got_right.at[block, m // 2],
@@ -227,13 +227,13 @@
 
                 r = s - away - hops
 
-                @pl.when((turn > 0) & (r >= 0) & (r < S - 2) & (r % 2 == c))
+                @pl.when((turn > 0) & (r >= 0) & (r < S - 4) & (r % 2 == c))
                 def _():
                     take(r, hops < G - 1)
 
                 n = s - away - hops + (G - 2) * (hops // (G - 1))
 
-                @pl.when((turn > 0) & (n >= S - 2) & (n < S) & (n % 2 == c))
+                @pl.when((turn > 0) & (n >= S - 4) & (n < S) & (n % 2 == c))
                 def _():
                     take(n, hops < G - 2)
 
@@ -246,7 +246,7 @@
         unit = last // (2 * group) * 2 + cycle
         done = jnp.minimum(last // (2 * group) * 2 + jnp.minimum(cycle, 2), 2 * units)
         for i in range(units):
-            ripe = 2 * (group * i + group - 1) + c + late - (i == units - 1)
+            ripe = 2 * (group * i + group - 1) + c + late - (i >= units - 2)
 
             @pl.when(s == ripe)
             def _():
@@ -289,7 +289,7 @@
         @pl.when(is_root)
         def _():
             sent(left.at[mine, pl.ds(0, pixels)], root_sem.at[zb])
-            sent(left.at[mine, pl.ds(0, 2 * rows)], both_sem.at[zb])
+            sent(left.at[mine, pl.ds(0, 4 * rows)], both_sem.at[zb])
 
         for e in range(2):
             block = 2 * zb + e
@@ -301,7 +301,7 @@
 
             @pl.when((turn > 0) & (hops == G - 2))
             def _():
-                sent(right.at[block, pl.ds(0, Q - rows)], ring_sem.at[block])
+                sent(right.at[block, pl.ds(0, Q - 2 * rows)], ring_sem.at[block])
 
 
 def finish_kernel(C, owned, fisher, left, weighted, scale, out, maps, columns, mine, out_sem, late_sem, maps_sem):

time: 77.9 us -> 78.1 us (level)
  the two profiles are of different devices: /device:TPU:6 before, /device:TPU:25 now
where the time goes in v6:
time: 78.1 us; the launch traced here: 77.9 us
  Pallas kernels  77.3 us (99%)
    pallas_call x1, Pallas kernels, shards(): pl.pallas_call(functools.partial(sky_kernel, G, C, rows, wide // rows), o...  69.8 us
    pallas_call x1, Pallas kernels, shards(): pl.pallas_call(functools.partial(finish_kernel, C, owned), out_shape=(jax...  7.47 us

profile of v6, /device:TPU:25, one launch (start us, length us, event | category | flops | bytes accessed | tf_op | source)
XLA Modules:
  0.0 77.9 jit_solution(17738886119385785502)
XLA Ops:
  0.6 69.8 %shard_map.59 = (f32[3072,768]{1,0:T(8,128)S(1)}, bf16[8,3200,128]{2,1,0:T(8,128)(2,1)S(1)}, bf16[1024,1536]{1,0:T(8,128)(2,1)S(1)}, f32[8,128]{1,0:T(8,128)S(1)}) custom-call(bf16[2,64,3072]{2,1,0:T(8,128)(2,1)} %bitcast.3, bf16[2,64,128]{2,1,0:T(8,128)(2,1)} %data_in.1, s32[4,128]{1,0:T(4,128)} %bitcast.5, f32[64,128]{1,0:T(8,128)} %bitcast.4), custom_call_target="tpu_custom_call" | custom-call | tf_op jit(solution)/shard_map/pallas_call | solution.py:363
  70.4 7.5 %shard_map.60 = (f32[3072,1536]{1,0:T(8,128)}, f32[384,128]{1,0:T(8,128)}) custom-call(f32[3072,768]{1,0:T(8,128)S(1)} %get-tuple-element.6.fisher, bf16[8,3200,128]{2,1,0:T(8,128)(2,1)S(1)} %get-tuple-element.7.left, bf16[1024,1536]{1,0:T(8,128)(2,1)S(1)} %get-tuple-element.8.weighted, f32[8,128]{1,0:T(8,128)S(1)} %get-tuple-element.9.scale), custom_call_target="tpu_custom_call" | custom-call | tf_op jit(solution)/shard_map/pallas_call | solution.py:381
